TPU v7x, 32 devices: a whole 2x2x4 slice. The times are simulated.
32 devices in a mesh: req: 16 (over z, x, core), mdl: 2 (over y).
Axes of the slice: x: 2, y: 2, z: 4, core: 2. Of those that a mesh axis runs over, the one named last changes fastest.
Arguments:
- hidden: bfloat16 [4096, 1536], P(('req', 'mdl')), may hold values from -6 to 6
- input_gain: float32 [1536], replicated, may hold values from 0.1 to 1.9
- gate_proj: bfloat16 [1536, 3072], P('req', 'mdl'), may hold values from -0.15625 to 0.15625
- value_proj: bfloat16 [1536, 3072], P('req', 'mdl'), may hold values from -0.15625 to 0.15625
- state_proj: bfloat16 [1536, 256], P('req'), may hold values from -0.15625 to 0.15625
- step_proj: bfloat16 [1536, 48], P('req', 'mdl'), may hold values from -0.15625 to 0.15625
- conv_value: float32 [5, 3072], P(None, 'mdl'), may hold values from -3 to 3
- conv_state: float32 [5, 256], replicated, may hold values from -3 to 3
- step_bias: float32 [48], P('mdl'), may hold values from -4 to -1
- decay_log: float32 [48], P('mdl'), may hold values from -4 to 0
- skip_gain: float32 [48], P('mdl'), may hold values from 0.5 to 1.5
- output_gain: float32 [3072], P('mdl'), may hold values from 0.1 to 1.9
- out_proj: bfloat16 [3072, 1536], P('mdl', 'req'), may hold values from -0.109375 to 0.109375
- state_start: float32 [32, 48, 64, 128], P('req', 'mdl'), may hold values from -0.8 to 0.8
- edge_value: bfloat16 [32, 3, 3072], P('req', None, 'mdl'), may hold values from -6 to 6
- edge_state: bfloat16 [32, 3, 256], P('req'), may hold values from -6 to 6
- lengths: int32 [32], P('req'), may hold values from 1 to 128, as said below
- accepted: int32 [32], P('req'), may hold values from 1 to 128, as said below
Outputs:
- mixed: bfloat16 [4096, 1536], P(('req', 'mdl'))
- state_final: float32 [32, 48, 64, 128], P(('req', 'mdl'))
- edge_final: bfloat16 [32, 3, 3328], P(('req', 'mdl'))
Inputs may be any that keep to these rules, and one draw needn't show every extreme that they name: `lengths`: one request's draft fills all 128 slots. accepted[r] <= lengths[r]; the request whose draft fills all slots accepts all of it.
All inputs are finite; a program needn't handle non-finite values.
Results may differ from a plain program's by a relative error of at most 0.009.
Values may be sent and summed in bfloat16 or wider, within the bound.
A program may use at most 64 MiB of HBM per device.

v0:
```python
import jax
import jax.numpy as jnp
from jax import lax
from jax.sharding import PartitionSpec as P

EPSILON = 1e-05
HIGHEST = lax.Precision.HIGHEST


def local(
    hidden,
    input_gain,
    gate_proj,
    value_proj,
    state_proj,
    step_proj,
    conv_value,
    conv_state,
    step_bias,
    decay_log,
    skip_gain,
    output_gain,
    out_proj,
    state_start,
    edge_value,
    edge_state,
    lengths,
    accepted,
):
    requests, heads_here, head_dim, nstate = state_start.shape
    rows_dev = hidden.shape[0]
    span = rows_dev * lax.axis_size("mdl") // requests
    here_count = rows_dev // span
    group_rows = requests * span
    inner_here = heads_here * head_dim
    width_k = conv_value.shape[0] - 1
    edge_count = width_k - 1
    my_index = lax.axis_index("mdl")
    floats = hidden.astype(jnp.float32)
    normed = (
        floats * lax.rsqrt(jnp.mean(floats * floats, -1, keepdims=True) + EPSILON) * input_gain
    ).astype(jnp.bfloat16)
    widths = (gate_proj.shape[1], value_proj.shape[1], state_proj.shape[1], step_proj.shape[1])
    first_end = widths[0]
    second_end = first_end + widths[1]
    third_end = second_end + widths[2]
    whole = lax.all_gather(normed, "mdl", axis=0, tiled=True)
    packed = jnp.concatenate((gate_proj, value_proj, state_proj, step_proj), 1)
    joined_piece = lax.all_gather(packed, "req", axis=0, tiled=True)
    joined = jnp.dot(whole, joined_piece, preferred_element_type=jnp.float32)
    gates = joined[:, :first_end].astype(jnp.bfloat16)
    values = joined[:, first_end:second_end].astype(jnp.bfloat16)
    readers = joined[:, second_end:third_end].astype(jnp.bfloat16)
    step_raw = joined[:, third_end:].astype(jnp.bfloat16)
    current = jnp.concatenate([values, readers], 1).reshape(requests, span, -1)
    edges = jnp.concatenate([edge_value, edge_state], 2)
    extended = jnp.concatenate([edges, current], 1).astype(jnp.float32)
    taps = jnp.concatenate([conv_value, conv_state], 1)
    convolved = taps[width_k][None, None, :] + jnp.zeros(
        (requests, span, taps.shape[1]), jnp.float32
    )
    for shift in range(width_k):
        convolved = convolved + taps[shift][None, None, :] * extended[:, shift : shift + span]
    active = jax.nn.silu(convolved).astype(jnp.bfloat16)
    vals = active[..., :inner_here].reshape(requests, span, heads_here, head_dim)
    inputs_b = active[..., inner_here : inner_here + nstate]
    reads_c = active[..., inner_here + nstate :]
    vals_f = vals.astype(jnp.float32)
    steps = jax.nn.softplus(
        step_raw.astype(jnp.float32).reshape(requests, span, heads_here) + step_bias
    )
    logs = -steps * jnp.exp(decay_log)
    sooner = jnp.arange(span, dtype=jnp.int32)
    triangle = (sooner[:, None] >= sooner[None, :]).astype(jnp.float32)
    running = jnp.einsum("ts,gsh->gth", triangle, logs, precision=HIGHEST)
    intersection = jnp.einsum("gtn,gsn->gts", reads_c, inputs_b, preferred_element_type=jnp.float32)
    positions = jnp.arange(span, dtype=jnp.int32)
    lower = positions[:, None] >= positions[None, :]
    spread = jnp.where(
        lower[None, :, :, None], running[:, :, None, :] - running[:, None, :, :], -jnp.inf
    )
    kernel = intersection[..., None] * jnp.exp(spread) * steps[:, None, :, :]
    outputs = jnp.einsum("gtsh,gshp->gthp", kernel, vals_f, precision=HIGHEST)
    carried = jnp.einsum(
        "gtn,ghpn->gthp", reads_c.astype(jnp.float32), state_start, precision=HIGHEST
    )
    outputs = outputs + jnp.exp(running)[..., None] * carried + skip_gain[:, None] * vals_f
    product = outputs.reshape(group_rows, inner_here) * jax.nn.silu(gates.astype(jnp.float32))
    squares = jnp.sum(product * product, -1)
    gated = (product * output_gain).astype(jnp.bfloat16)
    total_squares = lax.psum(squares, "mdl")
    scale = lax.rsqrt(total_squares / (inner_here * lax.axis_size("mdl")) + EPSILON)
    partial_terms = jnp.dot(
        gated,
        lax.all_gather(out_proj, "req", axis=1, tiled=True),
        preferred_element_type=jnp.float32,
    )
    mine = lax.psum_scatter(
        partial_terms.astype(jnp.bfloat16), "mdl", scatter_dimension=0, tiled=True
    ).astype(jnp.float32)
    my_scale = lax.dynamic_slice_in_dim(scale, my_index * rows_dev, rows_dev, 0)
    my_lengths = lax.dynamic_slice_in_dim(lengths, my_index * here_count, here_count, 0)
    live = (positions[None, :] < my_lengths[:, None]).reshape(rows_dev).astype(jnp.float32)
    mixed = (mine * my_scale[:, None] * live[:, None]).astype(jnp.bfloat16)
    last = accepted - 1
    chosen = (positions[None, :] == last[:, None]).astype(jnp.float32)
    running_last = jnp.sum(chosen[:, :, None] * running, axis=1)
    before = positions[None, :] <= last[:, None]
    reach = jnp.where(before[:, :, None], running_last[:, None, :] - running, -jnp.inf)
    weights_s = jnp.exp(reach) * steps
    gathered_state = jnp.einsum(
        "gsh,gshp,gsn->ghpn", weights_s, vals_f, inputs_b.astype(jnp.float32), precision=HIGHEST
    )
    state_here = jnp.exp(running_last)[:, :, None, None] * state_start + gathered_state
    picks = accepted[:, None] + jnp.arange(edge_count, dtype=jnp.int32)[None, :]
    selected = jnp.take_along_axis(extended, picks[:, :, None], axis=1)
    value_edges = selected[..., :inner_here].reshape(requests, edge_count, heads_here, head_dim)
    value_edges = value_edges.transpose(0, 2, 1, 3).reshape(
        requests, heads_here, edge_count * head_dim
    )
    states_home, edges_home = (
        lax.all_to_all(
            state_here.reshape(requests, heads_here, head_dim * nstate).astype(jnp.bfloat16),
            "mdl",
            split_axis=0,
            concat_axis=1,
            tiled=True,
        ).astype(jnp.float32),
        lax.all_to_all(
            value_edges.astype(jnp.bfloat16), "mdl", split_axis=0, concat_axis=1, tiled=True
        ).astype(value_edges.dtype),
    )
    heads_all = states_home.shape[1]
    state_final = states_home.reshape(here_count, heads_all, head_dim, nstate)
    edges_home = edges_home.reshape(here_count, heads_all, edge_count, head_dim).transpose(
        0, 2, 1, 3
    )
    edges_home = edges_home.reshape(here_count, edge_count, heads_all * head_dim)
    state_edges = lax.dynamic_slice_in_dim(
        selected[..., inner_here:], my_index * here_count, here_count, 0
    )
    edge_final = jnp.concatenate([edges_home, state_edges], 2).astype(jnp.bfloat16)
    return (mixed, state_final, edge_final)


def solution(mesh):
    return jax.shard_map(
        local,
        mesh=mesh,
        in_specs=(
            P(("req", "mdl"), None),
            P(),
            P("req", "mdl"),
            P("req", "mdl"),
            P("req", None),
            P("req", "mdl"),
            P(None, "mdl"),
            P(),
            P("mdl"),
            P("mdl"),
            P("mdl"),
            P("mdl"),
            P("mdl", "req"),
            P("req", "mdl", None, None),
            P("req", None, "mdl"),
            P("req", None, None),
            P("req"),
            P("req"),
        ),
        out_specs=(
            P(("req", "mdl"), None),
            P(("req", "mdl"), None, None, None),
            P(("req", "mdl"), None, None),
        ),
        check_vma=False,
    )
```

profile of v0, /device:TPU:0, one launch (start us, length us, event | category | flops | bytes accessed | tf_op | source)
XLA Modules:
  0.0 201.5 jit_solution(17263862476050745246)
XLA Ops:
  7.3 0.9 copy.52
  8.2 2.0 pad_maximum_fusion
  10.2 0.7 all-gather.5.cloned.1.call-update
  11.1 0.1 fusion.43
  11.1 0.1 reshape.272
  11.2 0.6 dynamic_slice.10
  11.8 0.6 compare_convert_fusion.1
  12.5 0.1 slice_reduce_fusion.4
  12.6 0.2 fusion.24
  12.8 0.2 fusion.26
  13.0 12.8 %all_gather.9 = bf16[256,1536]{1,0:T(8,128)(2,1)S(1)} all-gather(bf16[128,1536]{1,0:T(8,128)(2,1)S(1)} %fusion.26), channel_id=1, replica_groups=mesh['req'=16,'mdl'=2] {'mdl'}, dimensions={0}, use_global_device_ids=true | all-gather | bytes 1179648 | tf_op jit(solution)/shard_map/all_gather | solution.py:47
  25.8 0.1 compare_and_fusion
  25.8 0.1 iota_compare_fusion.2
  25.9 76.5 %all-gather.3.cloned.1.call-done = bf16[1536,3352]{1,0:T(8,128)(2,1)} async-done(((bf16[96,3352]{1,0:T(8,128)(2,1)}), bf16[1536,3352]{1,0:T(8,128)(2,1)}) %all-gather.3.cloned.1.call-update) | async-done | bytes 10297360 | tf_op jit(solution)/shard_map/all_gather | solution.py:49
  102.4 8.3 %convolution_convert_fusion = bf16[256,3352]{0,1:T(8,128)(2,1)S(1)} fusion(bf16[256,1536]{1,0:T(8,128)(2,1)S(1)} %all_gather.9, bf16[1536,3352]{1,0:T(8,128)(2,1)} %all-gather.3.cloned.1.call-done), kind=kOutput, calls=%fused_computation.1 | convolution fusion | flops 2636978176 | bytes 12800000 | tf_op jit(solution)/shard_map/dot_general | solution.py:50
  110.7 1.2 copy-done.3
  111.9 0.8 copy.63
  112.7 0.2 maximum_convert_fusion
  112.9 1.9 copy.57
  114.8 1.2 multiply_convert_fusion
  116.1 1.2 copy.54
  117.3 0.8 compare_select_fusion
  118.1 1.0 multiply_reduce_fusion.1
  119.1 0.8 exponential_multiply_fusion
  119.9 0.2 fusion.34
  120.1 0.8 fusion.30
  121.0 0.1 copy-done.2
  121.1 3.5 %fusion.10 = f32[2,128,24,64]{1,3,2,0:T(8,128)S(1)} fusion(bf16[2,128,24,64]{1,3,2,0:T(8,128)(2,1)S(1)} %bitcast.75, f32[2,128,24,64]{1,3,2,0:T(8,128)S(1)} %fusion.30, f32[2,128,24]{1,2,0:T(8,128)S(1)} %compare_select_fusion, f32[2,128,24]{1,2,0:T(8,128)S(1)} %get-tuple-element.13, f32[2,128,128]{2,1,0:T(8,128)S(1)} %fusion.34, ...), kind=kOutput, calls=%fused_computation.22 | convolution fusion | flops 609091584 | bytes 4153440 | tf_op jit(solution)/shard_map/gtsh,gshp->gthp/dot_general | solution.py:83
  124.6 1.2 copy.56
  125.8 30.4 %all-gather.5.cloned.1.call-done = bf16[1536,1536]{0,1:T(8,128)(2,1)} async-done(((bf16[1536,96]{0,1:T(8,128)(2,1)}), bf16[1536,1536]{0,1:T(8,128)(2,1)}) %all-gather.5.cloned.1.call-update) | async-done | bytes 4718608 | tf_op jit(solution)/shard_map/all_gather | solution.py:95
  156.2 5.3 %convolution_convert_fusion.1 = bf16[256,1536]{1,0:T(8,128)(2,1)} fusion(bf16[1536,1536]{0,1:T(8,128)(2,1)} %all-gather.5.cloned.1.call-done, f32[1536]{0:T(1024)S(1)} %copy-done.11, f32[192,8,2,128]{3,2,1,0:T(2,128)S(1)} %bitcast.71, bf16[256,3352]{0,1:T(8,128)(2,1)} %copy-done.3), kind=kOutput, calls=%fused_computation.8 | convolution fusion | flops 1211498496 | bytes 7870464 | tf_op jit(solution)/shard_map/dot_general | solution.py:93
  161.6 1.4 gather_fusion
  163.0 0.1 broadcast_select_fusion
  163.2 0.1 convert_element_type.121
  163.3 0.7 convert_element_type.123
  164.0 3.3 %all-to-all-start.1 = ((bf16[2,24,192]{2,1,0:T(8,128)(2,1)}), bf16[2,24,192]{2,1,0:T(8,128)(2,1)S(1)}, u32[]{:S(2)}, u32[]{:S(2)}) async-start(bf16[2,24,192]{2,1,0:T(8,128)(2,1)} %convert_element_type.123), calls=%async_computation.2 | async-start | bytes 49152 | tf_op jit(solution)/shard_map/all_to_all | solution.py:129
  167.3 1.7 multiply_reduce_fusion
  168.9 5.0 %psum.7 = f32[256]{0:T(256)S(1)} all-reduce(f32[256]{0:T(256)S(1)} %multiply_reduce_fusion), channel_id=1, replica_groups=mesh['req'=16,'mdl'=2] {'mdl'}, use_global_device_ids=true, to_apply=%region_3.4 | all-reduce | flops 256 | bytes 2048 | tf_op jit(solution)/shard_map/psum | solution.py:91
  173.9 2.1 %add_convert_fusion = bf16[2,24,64,128]{3,2,1,0:T(8,128)(2,1)S(1)} fusion(f32[2,24,64,128]{3,2,1,0:T(8,128)S(1)} %copy-done, bf16[2,128,24,64]{1,3,2,0:T(8,128)(2,1)} %bitcast.74, f32[2,128,24]{1,2,0:T(8,128)S(1)} %get-tuple-element.8, f32[2,24]{1,0:T(2,128)S(1)} %exp.41, bf16[2,128,1792]{2,1,0:T(8,128)(2,1)} %copy-done.1), kind=kOutput, calls=%fused_computation.29 | convolution fusion | flops 605945856 | bytes 3236032 | tf_op jit(solution)/shard_map/gsh,gshp,gsn->ghpn/dot_general | solution.py:111
  176.1 1.2 convert_element_type.118
  177.3 0.1 dynamic_slice.9
  177.4 3.5 %all-to-all-start = ((bf16[2,24,8192]{2,1,0:T(8,128)(2,1)}), bf16[2,24,8192]{2,1,0:T(8,128)(2,1)S(1)}, u32[]{:S(2)}, u32[]{:S(2)}) async-start(bf16[2,24,8192]{2,1,0:T(8,128)(2,1)} %convert_element_type.118), calls=%async_computation.1 | async-start | bytes 1572864 | tf_op jit(solution)/shard_map/all_to_all | solution.py:122
  180.9 0.1 convert_element_type.124
  181.0 0.1 concatenate.34
  181.1 0.6 pad_maximum_fusion.1
  181.8 9.9 %all-to-all-done = bf16[2,24,8192]{2,1,0:T(8,128)(2,1)S(1)} async-done(((bf16[2,24,8192]{2,1,0:T(8,128)(2,1)}), bf16[2,24,8192]{2,1,0:T(8,128)(2,1)S(1)}, u32[]{:S(2)}, u32[]{:S(2)}) %all-to-all-start) | async-done | bytes 786464 | tf_op jit(solution)/shard_map/all_to_all | solution.py:122
  191.7 1.3 copy.66
  193.0 2.0 multiply_convert_fusion.3
  (56 shorter events, 0.5 us)
Async XLA Ops:
  7.2 3.8 %copy-start.6 = (bf16[2,3,1536]{2,0,1:T(2,128)(2,1)S(1)}, bf16[2,3,1536]{2,0,1:T(2,128)(2,1)}, u32[]{:S(2)}) copy-start(bf16[2,3,1536]{2,0,1:T(2,128)(2,1)} %param.32) | copy-start | bytes 55300
  7.2 3.8 %copy-start.9 = (bf16[2,3,256]{2,0,1:T(2,128)(2,1)S(1)}, bf16[2,3,256]{2,0,1:T(2,128)(2,1)}, u32[]{:S(2)}) copy-start(bf16[2,3,256]{2,0,1:T(2,128)(2,1)} %param.33) | copy-start | bytes 9220
  7.2 3.8 %copy-start.12 = (f32[24]{0:T(128)S(1)}, f32[24]{0:T(128)}, u32[]{:S(2)}) copy-start(f32[24]{0:T(128)} %param.27) | copy-start | bytes 292
  7.2 3.9 %copy-start.14 = (s32[2]{0:T(128)S(1)}, s32[2]{0:T(128)}, u32[]{:S(2)}) copy-start(s32[2]{0:T(128)} %param.35) | copy-start | bytes 28
  7.2 4.0 %copy-start.13 = (s32[2]{0:T(128)S(1)}, s32[2]{0:T(128)}, u32[]{:S(2)}) copy-start(s32[2]{0:T(128)} %param.34) | copy-start | bytes 28
  7.2 5.3 %copy-start.5 = (f32[5,1536]{1,0:T(8,128)S(1)}, f32[5,1536]{1,0:T(8,128)}, u32[]{:S(2)}) copy-start(f32[5,1536]{1,0:T(8,128)} %param.24) | copy-start | bytes 92164
  7.2 5.3 %copy-start.8 = (f32[5,256]{1,0:T(8,128)S(1)}, f32[5,256]{1,0:T(8,128)}, u32[]{:S(2)}) copy-start(f32[5,256]{1,0:T(8,128)} %param.25) | copy-start | bytes 15364
  7.2 5.4 %copy-start.4 = (bf16[128,1536]{1,0:T(8,128)(2,1)S(1)}, bf16[128,1536]{1,0:T(8,128)(2,1)}, u32[]{:S(2)}) copy-start(bf16[128,1536]{1,0:T(8,128)(2,1)} %param.18) | copy-start | bytes 1179652
  7.2 5.6 %copy-start.7 = (f32[1536]{0:T(1024)S(1)}, f32[1536]{0:T(1024)}, u32[]{:S(2)}) copy-start(f32[1536]{0:T(1024)} %param.19) | copy-start | bytes 18436
  7.3 95.1 %all-gather.3.cloned.1.call-start = ((), (), s32[]{:S(2)}) async-start(), calls=%async_computation.3 | async-start | bytes 11280384 | tf_op jit(solution)/shard_map/all_gather | solution.py:49
  10.2 146.1 %all-gather.5.cloned.1.call-start = ((), (), s32[]{:S(2)}) async-start(), calls=%async_computation.4 | async-start | bytes 5013504 | tf_op jit(solution)/shard_map/all_gather | solution.py:95
  10.9 182.1 %reduce-scatter.2.cloned.1.call-start = ((), (), s32[]{:S(2)}) async-start(), calls=%async_computation.5 | async-start | bytes 1179648 | tf_op jit(solution)/shard_map/reduce_scatter | solution.py:98
  110.6 1.2 copy-start.3
  116.0 4.1 %copy-start.1 = (bf16[2,128,1792]{2,1,0:T(8,128)(2,1)}, bf16[2,128,1792]{2,1,0:T(8,128)(2,1)S(1)}, u32[]{:S(2)}) copy-start(bf16[2,128,1792]{2,1,0:T(8,128)(2,1)S(1)} %multiply_convert_fusion) | copy-start | bytes 2752516
  116.0 1.3 copy-start.10
  116.0 4.1 %copy-start = (f32[2,24,64,128]{3,2,1,0:T(8,128)S(1)}, f32[2,24,64,128]{3,2,1,0:T(8,128)}, u32[]{:S(2)}) copy-start(f32[2,24,64,128]{3,2,1,0:T(8,128)} %param.31) | copy-start | bytes 4718596
  119.9 1.1 copy-start.2
  119.9 1.1 copy-start.15
  124.6 31.7 %copy-start.11 = (f32[1536]{0:T(1024)S(1)}, f32[1536]{0:T(1024)}, u32[]{:S(2)}) copy-start(f32[1536]{0:T(1024)} %param.29) | copy-start | bytes 18436
  164.0 13.4 %all-to-all-start.1 = ((bf16[2,24,192]{2,1,0:T(8,128)(2,1)}), bf16[2,24,192]{2,1,0:T(8,128)(2,1)S(1)}, u32[]{:S(2)}, u32[]{:S(2)}) async-start(bf16[2,24,192]{2,1,0:T(8,128)(2,1)} %convert_element_type.123), calls=%async_computation.2 | async-start | bytes 49152 | tf_op jit(solution)/shard_map/all_to_all | solution.py:129
  177.4 14.3 %all-to-all-start = ((bf16[2,24,8192]{2,1,0:T(8,128)(2,1)}), bf16[2,24,8192]{2,1,0:T(8,128)(2,1)S(1)}, u32[]{:S(2)}, u32[]{:S(2)}) async-start(bf16[2,24,8192]{2,1,0:T(8,128)(2,1)} %convert_element_type.118), calls=%async_computation.1 | async-start | bytes 1572864 | tf_op jit(solution)/shard_map/all_to_all | solution.py:122
Sparse Core Ops, SparseCore 0:
  10.9 91.3 all-gather.2
  104.6 51.5 all-gather.4
  161.7 16.3 reduce-scatter.1
where the time goes:
time: 202 us
  waiting for transfers between devices  118 us (58%)
  matrix products  21.2 us (10%)
  blocking collectives  17.7 us (9%)
  between operations  14.2 us (7%)
  local copies, waits for them, and re-layouts  13.4 us (7%)
  other arithmetic  10.6 us (5%)
  starting transfers between devices  6.91 us (3%)
    all_gather x1, waiting for transfers between devices, local(): joined_piece = lax.all_gather(packed, 'req', axis=0, tiled=True)  76.5 us
    all_gather x1, waiting for transfers between devices, local(): lax.all_gather(out_proj, 'req', axis=1, tiled=True)  30.4 us
    all_gather x1, blocking collectives, local(): whole = lax.all_gather(normed, 'mdl', axis=0, tiled=True)  12.8 us
    all_to_all x1, waiting for transfers between devices, local(): lax.all_to_all(state_here.reshape(requests, heads_here, head_dim * nstate...  9.9 us
    dot_general x1, matrix products, local(): joined = jnp.dot(whole, joined_piece, preferred_element_type=jnp.float32)  8.28 us
    dot_general x1, matrix products, local(): jnp.dot(gated, lax.all_gather(out_proj, 'req', axis=1, tiled=True), prefe...  5.3 us
    psum x1, blocking collectives, local(): total_squares = lax.psum(squares, 'mdl')  4.99 us
  transfers between devices with their start and end apart: 5, of which 3 were waited for; matrix products, arithmetic and copies ran while one was open for 17% of the time, Pallas kernels for 0%

commit v1 on v0

--- a/solution.py
+++ b/solution.py
@@ -5,6 +5,28 @@
 
 EPSILON = 1e-05
 HIGHEST = lax.Precision.HIGHEST
+
+
+def laid_out(parts, dim):
+    dims = list(parts.shape[1:])
+    dims[dim] *= parts.shape[0]
+    return jnp.moveaxis(parts, 0, dim).reshape(dims)
+
+
+def collect(array, axis, dim):
+    peers = lax.axis_size(axis)
+    pairs = [(i, (i + 1) % peers) for i in range(peers)]
+    back = [(b, a) for a, b in pairs]
+    lower, upper = ([], [])
+    for turn in range(peers - 1):
+        if turn % 2 == 0:
+            lower.append(lax.ppermute(lower[-1] if lower else array, axis, pairs))
+        else:
+            upper.append(lax.ppermute(upper[-1] if upper else array, axis, back))
+    parts = jnp.stack([*lower[::-1], array, *upper])
+    shift = lax.axis_index(axis) - len(lower)
+    parts = parts[(jnp.arange(peers) - shift) % peers]
+    return laid_out(parts, dim)
 
 
 def local(
@@ -46,7 +68,7 @@
     third_end = second_end + widths[2]
     whole = lax.all_gather(normed, "mdl", axis=0, tiled=True)
     packed = jnp.concatenate((gate_proj, value_proj, state_proj, step_proj), 1)
-    joined_piece = lax.all_gather(packed, "req", axis=0, tiled=True)
+    joined_piece = collect(packed, "req", 0)
     joined = jnp.dot(whole, joined_piece, preferred_element_type=jnp.float32)
     gates = joined[:, :first_end].astype(jnp.bfloat16)
     values = joined[:, first_end:second_end].astype(jnp.bfloat16)

time: 202 us -> 252 us (1.25)
  starting transfers between devices: 6.91 us -> 77.5 us
  waiting for transfers between devices: 118 us -> 60.5 us
  local copies, waits for them, and re-layouts: 13.4 us -> 47.3 us
  other arithmetic: 10.6 us -> 13.5 us
    all_gather x1 -> x0, waiting for transfers between devices: 76.5 us -> none  [local(): joined_piece = lax.all_gather(packed, 'req', axis=0, tiled=True)]
    ppermute x0 -> x15, starting transfers between devices: none -> 70.6 us  [the longest x8 62.8 us: collect(): lower.append(lax.ppermute(lower[-1] if lower else array, axis, pairs))]
    ppermute x0 -> x15, waiting for transfers between devices: none -> 49.1 us  [the longest x8 49.1 us: collect(): lower.append(lax.ppermute(lower[-1] if lower else array, axis, pairs))]
    all_gather x1, waiting for transfers between devices: 30.4 us -> 0.02 us  [local(): lax.all_gather(out_proj, 'req', axis=1, tiled=True)]
    unnamed x37 -> x69, local copies, waits for them, and re-layouts: 3.61 us -> 24.5 us
    gather x0 -> x1, local copies, waits for them, and re-layouts: none -> 9.84 us  [collect(): parts = parts[(jnp.arange(peers) - shift) % peers]]
  transfers between devices with their start and end apart: 5 -> 19, of which waited for: 3 -> 8; matrix products, arithmetic and copies ran while one was open for 17% -> 28% of each run, Pallas kernels for 0% -> 0%
where the time goes in v1:
time: 252 us; the launch traced here: 251 us
  starting transfers between devices  77.5 us (31%)
  waiting for transfers between devices  60.5 us (24%)
  local copies, waits for them, and re-layouts  47.3 us (19%)
  matrix products  21.4 us (8%)
  blocking collectives  16 us (6%)
  between operations  14.6 us (6%)
  other arithmetic  13.5 us (5%)
    ppermute x8, starting transfers between devices, collect(): lower.append(lax.ppermute(lower[-1] if lower else array, axis, pairs))  62.8 us
    ppermute x8, waiting for transfers between devices, collect(): lower.append(lax.ppermute(lower[-1] if lower else array, axis, pairs))  49.1 us
    unnamed x69, local copies, waits for them, and re-layouts  24.5 us
    all_to_all x1, waiting for transfers between devices, local(): lax.all_to_all(state_here.reshape(requests, heads_here, head_dim * nstate...  11.4 us
    all_gather x1, blocking collectives, local(): whole = lax.all_gather(normed, 'mdl', axis=0, tiled=True)  11.1 us
    gather x1, local copies, waits for them, and re-layouts, collect(): parts = parts[(jnp.arange(peers) - shift) % peers]  9.84 us
    dot_general x1, matrix products, local(): joined = jnp.dot(whole, joined_piece, preferred_element_type=jnp.float32)  8.28 us
    ppermute x7, starting transfers between devices, collect(): upper.append(lax.ppermute(upper[-1] if upper else array, axis, back))  7.86 us
  transfers between devices with their start and end apart: 19, of which 8 were waited for; matrix products, arithmetic and copies ran while one was open for 28% of the time, Pallas kernels for 0%

profile of v1, /device:TPU:0, one launch (start us, length us, event | category | flops | bytes accessed | tf_op | source)
XLA Modules:
  0.0 250.8 jit_solution(1904856078289133528)
XLA Ops:
  8.2 1.1 pad_maximum_fusion
  9.8 13.3 %collective-permute-done = bf16[96,3352]{1,0:T(8,128)(2,1)S(1)} collective-permute-done((bf16[96,3352]{1,0:T(8,128)(2,1)S(1)}, bf16[96,3352]{1,0:T(8,128)(2,1)S(1)}, u32[]{:S(2)}, u32[]{:S(2)}) %collective-permute-start) | collective-permute-done | bytes 643616 | tf_op jit(solution)/shard_map/ppermute | solution.py:23
  23.1 4.4 %collective-permute-start.8 = (bf16[96,3352]{1,0:T(8,128)(2,1)S(1)}, bf16[96,3352]{1,0:T(8,128)(2,1)S(1)}, u32[]{:S(2)}, u32[]{:S(2)}) collective-permute-start(bf16[96,3352]{1,0:T(8,128)(2,1)S(1)} %pad_maximum_fusion), channel_id=1, source_target_pairs={{2,0},{4,2},{6,4},{8,6},{10,8},{12,10},{14,12},{16,14},{18,16},{20... | collective-permute-start | bytes 1930760 | tf_op jit(solution)/shard_map/ppermute | solution.py:25
  27.6 8.5 %collective-permute-done.1 = bf16[96,3352]{1,0:T(8,128)(2,1)S(1)} collective-permute-done((bf16[96,3352]{1,0:T(8,128)(2,1)S(1)}, bf16[96,3352]{1,0:T(8,128)(2,1)S(1)}, u32[]{:S(2)}, u32[]{:S(2)}) %collective-permute-start.1) | collective-permute-done | bytes 643616 | tf_op jit(solution)/shard_map/ppermute | solution.py:23
  36.0 1.2 collective-permute-start.2
  37.2 3.2 %collective-permute-start.9 = (bf16[96,3352]{1,0:T(8,128)(2,1)S(1)}, bf16[96,3352]{1,0:T(8,128)(2,1)S(1)}, u32[]{:S(2)}, u32[]{:S(2)}) collective-permute-start(bf16[96,3352]{1,0:T(8,128)(2,1)S(1)} %collective-permute-done.8), channel_id=1, source_target_pairs={{2,0},{4,2},{6,4},{8,6},{10,8},{12,10},{14,12},{16,14},{18,16},{20... | collective-permute-start | bytes 1930760 | tf_op jit(solution)/shard_map/ppermute | solution.py:25
  40.5 8.6 %collective-permute-done.2 = bf16[96,3352]{1,0:T(8,128)(2,1)} collective-permute-done((bf16[96,3352]{1,0:T(8,128)(2,1)S(1)}, bf16[96,3352]{1,0:T(8,128)(2,1)}, u32[]{:S(2)}, u32[]{:S(2)}) %collective-permute-start.2) | collective-permute-done | bytes 643616 | tf_op jit(solution)/shard_map/ppermute | solution.py:23
  49.0 4.6 %collective-permute-start.3 = (bf16[96,3352]{1,0:T(8,128)(2,1)}, bf16[96,3352]{1,0:T(8,128)(2,1)}, u32[]{:S(2)}, u32[]{:S(2)}) collective-permute-start(bf16[96,3352]{1,0:T(8,128)(2,1)} %collective-permute-done.2), channel_id=1, source_target_pairs={{0,2},{2,4},{4,6},{6,8},{8,10},{10,12},{12,14},{14,16},{16,18},{18... | collective-permute-start | bytes 1930760 | tf_op jit(solution)/shard_map/ppermute | solution.py:23
  53.7 1.2 dynamic_slice.10
  55.1 7.2 %collective-permute-done.3 = bf16[96,3352]{1,0:T(8,128)(2,1)} collective-permute-done((bf16[96,3352]{1,0:T(8,128)(2,1)}, bf16[96,3352]{1,0:T(8,128)(2,1)}, u32[]{:S(2)}, u32[]{:S(2)}) %collective-permute-start.3) | collective-permute-done | bytes 643616 | tf_op jit(solution)/shard_map/ppermute | solution.py:23
  62.2 12.2 %collective-permute-start.4 = (bf16[96,3352]{1,0:T(8,128)(2,1)}, bf16[96,3352]{1,0:T(8,128)(2,1)S(1)}, u32[]{:S(2)}, u32[]{:S(2)}) collective-permute-start(bf16[96,3352]{1,0:T(8,128)(2,1)} %collective-permute-done.3), channel_id=1, source_target_pairs={{0,2},{2,4},{4,6},{6,8},{8,10},{10,12},{12,14},{14,16},{16,18},{18... | collective-permute-start | bytes 1930760 | tf_op jit(solution)/shard_map/ppermute | solution.py:23
  77.6 6.5 %collective-permute-done.4 = bf16[96,3352]{1,0:T(8,128)(2,1)S(1)} collective-permute-done((bf16[96,3352]{1,0:T(8,128)(2,1)}, bf16[96,3352]{1,0:T(8,128)(2,1)S(1)}, u32[]{:S(2)}, u32[]{:S(2)}) %collective-permute-start.4) | collective-permute-done | bytes 643616 | tf_op jit(solution)/shard_map/ppermute | solution.py:23
  84.1 13.1 %collective-permute-start.5 = (bf16[96,3352]{1,0:T(8,128)(2,1)S(1)}, bf16[96,3352]{1,0:T(8,128)(2,1)}, u32[]{:S(2)}, u32[]{:S(2)}) collective-permute-start(bf16[96,3352]{1,0:T(8,128)(2,1)S(1)} %collective-permute-done.4), channel_id=1, source_target_pairs={{0,2},{2,4},{4,6},{6,8},{8,10},{10,12},{12,14},{14,16},{16,18},{18... | collective-permute-start | bytes 1930760 | tf_op jit(solution)/shard_map/ppermute | solution.py:23
  97.9 5.0 %collective-permute-done.5 = bf16[96,3352]{1,0:T(8,128)(2,1)} collective-permute-done((bf16[96,3352]{1,0:T(8,128)(2,1)S(1)}, bf16[96,3352]{1,0:T(8,128)(2,1)}, u32[]{:S(2)}, u32[]{:S(2)}) %collective-permute-start.5) | collective-permute-done | bytes 643616 | tf_op jit(solution)/shard_map/ppermute | solution.py:23
  102.9 15.9 %collective-permute-start.6 = (bf16[96,3352]{1,0:T(8,128)(2,1)}, bf16[96,3352]{1,0:T(8,128)(2,1)}, u32[]{:S(2)}, u32[]{:S(2)}) collective-permute-start(bf16[96,3352]{1,0:T(8,128)(2,1)} %collective-permute-done.5), channel_id=1, source_target_pairs={{0,2},{2,4},{4,6},{6,8},{8,10},{10,12},{12,14},{14,16},{16,18},{18... | collective-permute-start | bytes 1930760 | tf_op jit(solution)/shard_map/ppermute | solution.py:23
  118.7 1.2 compare_convert_fusion.1
  121.1 15.3 %collective-permute-start.7 = (bf16[96,3352]{1,0:T(8,128)(2,1)}, bf16[96,3352]{1,0:T(8,128)(2,1)S(1)}, u32[]{:S(2)}, u32[]{:S(2)}) collective-permute-start(bf16[96,3352]{1,0:T(8,128)(2,1)} %collective-permute-done.6), channel_id=1, source_target_pairs={{0,2},{2,4},{4,6},{6,8},{8,10},{10,12},{12,14},{14,16},{16,18},{18... | collective-permute-start | bytes 1930760 | tf_op jit(solution)/shard_map/ppermute | solution.py:23
  136.4 11.1 %all_gather.6 = bf16[256,1536]{1,0:T(8,128)(2,1)S(1)} all-gather(bf16[128,1536]{1,0:T(8,128)(2,1)S(1)} %fusion.26), channel_id=1, replica_groups=mesh['req'=16,'mdl'=2] {'mdl'}, dimensions={0}, use_global_device_ids=true | all-gather | bytes 1179648 | tf_op jit(solution)/shard_map/all_gather | solution.py:69
  148.8 0.9 bitcast_dynamic-update-slice_fusion.15
  149.7 2.0 bitcast_dynamic-update-slice_fusion.14
  151.7 2.0 bitcast_dynamic-update-slice_fusion.13
  154.6 2.0 bitcast_dynamic-update-slice_fusion.11
  156.5 2.0 bitcast_dynamic-update-slice_fusion.10
  160.4 0.9 bitcast_dynamic-update-slice_fusion.7
  163.1 0.9 bitcast_dynamic-update-slice_fusion.4
  164.0 2.0 bitcast_dynamic-update-slice_fusion.3
  166.0 2.0 bitcast_dynamic-update-slice_fusion.2
  168.9 0.9 bitcast_dynamic-update-slice_fusion
  169.8 9.8 %gather_fusion = bf16[16,96,3352]{2,1,0:T(8,128)(2,1)} fusion(bf16[16,96,3352]{2,1,0:T(8,128)(2,1)} %bitcast_dynamic-update-slice_fusion, s32[1024]{0:T(1024)} %pad_clamp_fusion), kind=kCustom, calls=%fused_computation | custom fusion | bytes 20594752 | tf_op jit(solution)/shard_map/gather | solution.py:28
  179.7 8.3 %convolution_convert_fusion = bf16[256,3352]{0,1:T(8,128)(2,1)S(1)} fusion(bf16[256,1536]{1,0:T(8,128)(2,1)S(1)} %all_gather.6, bf16[1536,3352]{1,0:T(8,128)(2,1)} %bitcast.106), kind=kOutput, calls=%fused_computation.2 | convolution fusion | flops 2636978176 | bytes 12800000 | tf_op jit(solution)/shard_map/dot_general | solution.py:72
  188.0 1.2 copy-done.3
  190.3 1.0 copy.57
  191.9 1.2 multiply_convert_fusion
  193.1 0.9 slice.92
  194.1 2.5 copy.54
  197.4 1.1 multiply_reduce_fusion.1
  200.3 3.5 %fusion.10 = f32[2,128,24,64]{1,3,2,0:T(8,128)S(1)} fusion(bf16[2,128,24,64]{1,3,2,0:T(8,128)(2,1)S(1)} %bitcast.111, f32[2,128,24,64]{1,3,2,0:T(8,128)S(1)} %fusion.30, f32[2,128,24]{1,2,0:T(8,128)S(1)} %compare_select_fusion, f32[2,128,24]{1,2,0:T(8,128)S(1)} %get-tuple-element.13, f32[2,128,128]{2,1,0:T(8,128)S(1)} %fusion.34, ...), kind=kOutput, calls=%fused_computation.23 | convolution fusion | flops 609091584 | bytes 4153440 | tf_op jit(solution)/shard_map/gtsh,gshp->gthp/dot_general | solution.py:105
  203.9 1.2 copy.56
  205.2 5.3 %convolution_convert_fusion.1 = bf16[256,1536]{1,0:T(8,128)(2,1)} fusion(bf16[1536,1536]{0,1:T(8,128)(2,1)} %all-gather.2.cloned.1.call-done, f32[1536]{0:T(1024)S(1)} %copy-done.20, f32[192,8,2,128]{3,2,1,0:T(2,128)S(1)} %bitcast.107, bf16[256,3352]{0,1:T(8,128)(2,1)} %copy-done.3), kind=kOutput, calls=%fused_computation.9 | convolution fusion | flops 1211498496 | bytes 7870464 | tf_op jit(solution)/shard_map/dot_general | solution.py:115
  211.5 3.2 %all-to-all-start.1 = ((bf16[2,24,192]{2,1,0:T(8,128)(2,1)}), bf16[2,24,192]{2,1,0:T(8,128)(2,1)S(1)}, u32[]{:S(2)}, u32[]{:S(2)}) async-start(bf16[2,24,192]{2,1,0:T(8,128)(2,1)} %convert_element_type.123), calls=%async_computation.2 | async-start | bytes 49152 | tf_op jit(solution)/shard_map/all_to_all | solution.py:151
  214.7 1.7 multiply_reduce_fusion
  216.4 4.9 %psum.7 = f32[256]{0:T(256)S(1)} all-reduce(f32[256]{0:T(256)S(1)} %multiply_reduce_fusion), channel_id=1, replica_groups=mesh['req'=16,'mdl'=2] {'mdl'}, use_global_device_ids=true, to_apply=%region_3.4 | all-reduce | flops 256 | bytes 2048 | tf_op jit(solution)/shard_map/psum | solution.py:113
  221.3 2.2 add_convert_fusion
  223.6 1.2 convert_element_type.118
  224.9 3.5 %all-to-all-start = ((bf16[2,24,8192]{2,1,0:T(8,128)(2,1)}), bf16[2,24,8192]{2,1,0:T(8,128)(2,1)S(1)}, u32[]{:S(2)}, u32[]{:S(2)}) async-start(bf16[2,24,8192]{2,1,0:T(8,128)(2,1)} %convert_element_type.118), calls=%async_computation.1 | async-start | bytes 1572864 | tf_op jit(solution)/shard_map/all_to_all | solution.py:144
  229.2 11.4 %all-to-all-done = bf16[2,24,8192]{2,1,0:T(8,128)(2,1)S(1)} async-done(((bf16[2,24,8192]{2,1,0:T(8,128)(2,1)}), bf16[2,24,8192]{2,1,0:T(8,128)(2,1)S(1)}, u32[]{:S(2)}, u32[]{:S(2)}) %all-to-all-start) | async-done | bytes 786464 | tf_op jit(solution)/shard_map/all_to_all | solution.py:144
  240.6 1.3 copy.66
  242.0 2.0 multiply_convert_fusion.3
  (120 shorter events, 19.4 us)
Async XLA Ops:
  7.2 69.4 %copy-start.4 = (bf16[128,1536]{1,0:T(8,128)(2,1)S(1)}, bf16[128,1536]{1,0:T(8,128)(2,1)}, u32[]{:S(2)}) copy-start(bf16[128,1536]{1,0:T(8,128)(2,1)} %param.18) | copy-start | bytes 1179652
  7.2 90.0 %copy-start.22 = (s32[2]{0:T(128)S(1)}, s32[2]{0:T(128)}, u32[]{:S(2)}) copy-start(s32[2]{0:T(128)} %param.35) | copy-start | bytes 28
  7.2 112.8 %copy-start.12 = (bf16[2,3,1536]{2,0,1:T(2,128)(2,1)S(1)}, bf16[2,3,1536]{2,0,1:T(2,128)(2,1)}, u32[]{:S(2)}) copy-start(bf16[2,3,1536]{2,0,1:T(2,128)(2,1)} %param.32) | copy-start | bytes 55300
  7.2 112.8 %copy-start.14 = (bf16[2,3,256]{2,0,1:T(2,128)(2,1)S(1)}, bf16[2,3,256]{2,0,1:T(2,128)(2,1)}, u32[]{:S(2)}) copy-start(bf16[2,3,256]{2,0,1:T(2,128)(2,1)} %param.33) | copy-start | bytes 9220
  7.2 112.9 %copy-start.21 = (f32[24]{0:T(128)S(1)}, f32[24]{0:T(128)}, u32[]{:S(2)}) copy-start(f32[24]{0:T(128)} %param.27) | copy-start | bytes 292
  7.2 113.5 %copy-start.13 = (f32[1536]{0:T(1024)S(1)}, f32[1536]{0:T(1024)}, u32[]{:S(2)}) copy-start(f32[1536]{0:T(1024)} %param.19) | copy-start | bytes 18436
  7.2 197.9 %all-gather.2.cloned.1.call-start = ((), (), s32[]{:S(2)}) async-start(), calls=%async_computation.3 | async-start | bytes 5013504 | tf_op jit(solution)/shard_map/all_gather | solution.py:117
  9.3 13.8 %collective-permute-start = (bf16[96,3352]{1,0:T(8,128)(2,1)S(1)}, bf16[96,3352]{1,0:T(8,128)(2,1)S(1)}, u32[]{:S(2)}, u32[]{:S(2)}) collective-permute-start(bf16[96,3352]{1,0:T(8,128)(2,1)S(1)} %pad_maximum_fusion), channel_id=1, source_target_pairs={{0,2},{2,4},{4,6},{6,8},{8,10},{10,12},{12,14},{14,16},{16,18},{18... | collective-permute-start | bytes 1930760 | tf_op jit(solution)/shard_map/ppermute | solution.py:23
  23.1 12.9 %collective-permute-start.1 = (bf16[96,3352]{1,0:T(8,128)(2,1)S(1)}, bf16[96,3352]{1,0:T(8,128)(2,1)S(1)}, u32[]{:S(2)}, u32[]{:S(2)}) collective-permute-start(bf16[96,3352]{1,0:T(8,128)(2,1)S(1)} %collective-permute-done), channel_id=1, source_target_pairs={{0,2},{2,4},{4,6},{6,8},{8,10},{10,12},{12,14},{14,16},{16,18},{18... | collective-permute-start | bytes 1930760 | tf_op jit(solution)/shard_map/ppermute | solution.py:23
  23.1 14.1 %collective-permute-start.8 = (bf16[96,3352]{1,0:T(8,128)(2,1)S(1)}, bf16[96,3352]{1,0:T(8,128)(2,1)S(1)}, u32[]{:S(2)}, u32[]{:S(2)}) collective-permute-start(bf16[96,3352]{1,0:T(8,128)(2,1)S(1)} %pad_maximum_fusion), channel_id=1, source_target_pairs={{2,0},{4,2},{6,4},{8,6},{10,8},{12,10},{14,12},{16,14},{18,16},{20... | collective-permute-start | bytes 1930760 | tf_op jit(solution)/shard_map/ppermute | solution.py:25
  36.0 13.0 %collective-permute-start.2 = (bf16[96,3352]{1,0:T(8,128)(2,1)S(1)}, bf16[96,3352]{1,0:T(8,128)(2,1)}, u32[]{:S(2)}, u32[]{:S(2)}) collective-permute-start(bf16[96,3352]{1,0:T(8,128)(2,1)S(1)} %collective-permute-done.1), channel_id=1, source_target_pairs={{0,2},{2,4},{4,6},{6,8},{8,10},{10,12},{12,14},{14,16},{16,18},{18... | collective-permute-start | bytes 1930760 | tf_op jit(solution)/shard_map/ppermute | solution.py:23
  37.2 17.8 %collective-permute-start.9 = (bf16[96,3352]{1,0:T(8,128)(2,1)S(1)}, bf16[96,3352]{1,0:T(8,128)(2,1)S(1)}, u32[]{:S(2)}, u32[]{:S(2)}) collective-permute-start(bf16[96,3352]{1,0:T(8,128)(2,1)S(1)} %collective-permute-done.8), channel_id=1, source_target_pairs={{2,0},{4,2},{6,4},{8,6},{10,8},{12,10},{14,12},{16,14},{18,16},{20... | collective-permute-start | bytes 1930760 | tf_op jit(solution)/shard_map/ppermute | solution.py:25
  49.0 13.2 %collective-permute-start.3 = (bf16[96,3352]{1,0:T(8,128)(2,1)}, bf16[96,3352]{1,0:T(8,128)(2,1)}, u32[]{:S(2)}, u32[]{:S(2)}) collective-permute-start(bf16[96,3352]{1,0:T(8,128)(2,1)} %collective-permute-done.2), channel_id=1, source_target_pairs={{0,2},{2,4},{4,6},{6,8},{8,10},{10,12},{12,14},{14,16},{16,18},{18... | collective-permute-start | bytes 1930760 | tf_op jit(solution)/shard_map/ppermute | solution.py:23
  53.7 188.3 %reduce-scatter.2.cloned.1.call-start = ((), (), s32[]{:S(2)}) async-start(), calls=%async_computation.4 | async-start | bytes 1179648 | tf_op jit(solution)/shard_map/reduce_scatter | solution.py:120
  55.0 21.7 %collective-permute-start.10 = (bf16[96,3352]{1,0:T(8,128)(2,1)S(1)}, bf16[96,3352]{1,0:T(8,128)(2,1)S(1)}, u32[]{:S(2)}, u32[]{:S(2)}) collective-permute-start(bf16[96,3352]{1,0:T(8,128)(2,1)S(1)} %collective-permute-done.9), channel_id=1, source_target_pairs={{2,0},{4,2},{6,4},{8,6},{10,8},{12,10},{14,12},{16,14},{18,16},{20... | collective-permute-start | bytes 1930760 | tf_op jit(solution)/shard_map/ppermute | solution.py:25
  62.2 21.9 %collective-permute-start.4 = (bf16[96,3352]{1,0:T(8,128)(2,1)}, bf16[96,3352]{1,0:T(8,128)(2,1)S(1)}, u32[]{:S(2)}, u32[]{:S(2)}) collective-permute-start(bf16[96,3352]{1,0:T(8,128)(2,1)} %collective-permute-done.3), channel_id=1, source_target_pairs={{0,2},{2,4},{4,6},{6,8},{8,10},{10,12},{12,14},{14,16},{16,18},{18... | collective-permute-start | bytes 1930760 | tf_op jit(solution)/shard_map/ppermute | solution.py:23
  76.7 0.8 copy-start.7
  77.6 20.2 %collective-permute-start.11 = (bf16[96,3352]{1,0:T(8,128)(2,1)S(1)}, bf16[96,3352]{1,0:T(8,128)(2,1)}, u32[]{:S(2)}, u32[]{:S(2)}) collective-permute-start(bf16[96,3352]{1,0:T(8,128)(2,1)S(1)} %collective-permute-done.10), channel_id=1, source_target_pairs={{2,0},{4,2},{6,4},{8,6},{10,8},{12,10},{14,12},{16,14},{18,16},{20... | collective-permute-start | bytes 1930760 | tf_op jit(solution)/shard_map/ppermute | solution.py:25
  84.1 13.7 %copy-start.9 = (bf16[96,3352]{1,0:T(8,128)(2,1)}, bf16[96,3352]{1,0:T(8,128)(2,1)S(1)}, u32[]{:S(2)}) copy-start(bf16[96,3352]{1,0:T(8,128)(2,1)S(1)} %collective-permute-done.4) | copy-start | bytes 1930756
  84.1 18.8 %collective-permute-start.5 = (bf16[96,3352]{1,0:T(8,128)(2,1)S(1)}, bf16[96,3352]{1,0:T(8,128)(2,1)}, u32[]{:S(2)}, u32[]{:S(2)}) collective-permute-start(bf16[96,3352]{1,0:T(8,128)(2,1)S(1)} %collective-permute-done.4), channel_id=1, source_target_pairs={{0,2},{2,4},{4,6},{6,8},{8,10},{10,12},{12,14},{14,16},{16,18},{18... | collective-permute-start | bytes 1930760 | tf_op jit(solution)/shard_map/ppermute | solution.py:23
  97.8 23.1 %collective-permute-start.12 = (bf16[96,3352]{1,0:T(8,128)(2,1)}, bf16[96,3352]{1,0:T(8,128)(2,1)}, u32[]{:S(2)}, u32[]{:S(2)}) collective-permute-start(bf16[96,3352]{1,0:T(8,128)(2,1)} %collective-permute-done.11), channel_id=1, source_target_pairs={{2,0},{4,2},{6,4},{8,6},{10,8},{12,10},{14,12},{16,14},{18,16},{20... | collective-permute-start | bytes 1930760 | tf_op jit(solution)/shard_map/ppermute | solution.py:25
  102.9 18.2 %collective-permute-start.6 = (bf16[96,3352]{1,0:T(8,128)(2,1)}, bf16[96,3352]{1,0:T(8,128)(2,1)}, u32[]{:S(2)}, u32[]{:S(2)}) collective-permute-start(bf16[96,3352]{1,0:T(8,128)(2,1)} %collective-permute-done.5), channel_id=1, source_target_pairs={{0,2},{2,4},{4,6},{6,8},{8,10},{10,12},{12,14},{14,16},{16,18},{18... | collective-permute-start | bytes 1930760 | tf_op jit(solution)/shard_map/ppermute | solution.py:23
  120.9 27.8 %collective-permute-start.13 = (bf16[96,3352]{1,0:T(8,128)(2,1)}, bf16[96,3352]{1,0:T(8,128)(2,1)S(1)}, u32[]{:S(2)}, u32[]{:S(2)}) collective-permute-start(bf16[96,3352]{1,0:T(8,128)(2,1)} %collective-permute-done.12), channel_id=1, source_target_pairs={{2,0},{4,2},{6,4},{8,6},{10,8},{12,10},{14,12},{16,14},{18,16},{20... | collective-permute-start | bytes 1930760 | tf_op jit(solution)/shard_map/ppermute | solution.py:25
  121.1 27.7 %collective-permute-start.7 = (bf16[96,3352]{1,0:T(8,128)(2,1)}, bf16[96,3352]{1,0:T(8,128)(2,1)S(1)}, u32[]{:S(2)}, u32[]{:S(2)}) collective-permute-start(bf16[96,3352]{1,0:T(8,128)(2,1)} %collective-permute-done.6), channel_id=1, source_target_pairs={{0,2},{2,4},{4,6},{6,8},{8,10},{10,12},{12,14},{14,16},{16,18},{18... | collective-permute-start | bytes 1930760 | tf_op jit(solution)/shard_map/ppermute | solution.py:23
  148.7 4.9 %copy-start.10 = (bf16[96,3352]{1,0:T(8,128)(2,1)S(1)}, bf16[96,3352]{1,0:T(8,128)(2,1)}, u32[]{:S(2)}) copy-start(bf16[96,3352]{1,0:T(8,128)(2,1)} %copy-done.9) | copy-start | bytes 1930756
  148.7 20.2 %collective-permute-start.14 = (bf16[96,3352]{1,0:T(8,128)(2,1)S(1)}, bf16[96,3352]{1,0:T(8,128)(2,1)S(1)}, u32[]{:S(2)}, u32[]{:S(2)}) collective-permute-start(bf16[96,3352]{1,0:T(8,128)(2,1)S(1)} %collective-permute-done.13), channel_id=1, source_target_pairs={{2,0},{4,2},{6,4},{8,6},{10,8},{12,10},{14,12},{16,14},{18,16},{20... | collective-permute-start | bytes 1930760 | tf_op jit(solution)/shard_map/ppermute | solution.py:25
  156.5 3.8 %copy-start.5 = (bf16[96,1536]{1,0:T(8,128)(2,1)S(1)}, bf16[96,1536]{1,0:T(8,128)(2,1)}, u32[]{:S(2)}) copy-start(bf16[96,1536]{1,0:T(8,128)(2,1)} %param.21) | copy-start | bytes 884740
  156.5 3.8 %copy-start.6 = (bf16[96,1536]{1,0:T(8,128)(2,1)S(1)}, bf16[96,1536]{1,0:T(8,128)(2,1)}, u32[]{:S(2)}) copy-start(bf16[96,1536]{1,0:T(8,128)(2,1)} %param.20) | copy-start | bytes 884740
  156.5 3.8 %copy-start.11 = (bf16[96,256]{1,0:T(8,128)(2,1)S(1)}, bf16[96,256]{1,0:T(8,128)(2,1)}, u32[]{:S(2)}) copy-start(bf16[96,256]{1,0:T(8,128)(2,1)} %param.22) | copy-start | bytes 147460
  160.4 2.7 %copy-start.8 = (bf16[96,3352]{1,0:T(8,128)(2,1)S(1)}, bf16[96,3352]{1,0:T(8,128)(2,1)}, u32[]{:S(2)}) copy-start(bf16[96,3352]{1,0:T(8,128)(2,1)} %copy-done.7) | copy-start | bytes 1930756
  188.0 1.2 copy-start.3
  193.1 6.4 %copy-start.1 = (bf16[2,128,1792]{2,1,0:T(8,128)(2,1)}, bf16[2,128,1792]{2,1,0:T(8,128)(2,1)S(1)}, u32[]{:S(2)}) copy-start(bf16[2,128,1792]{2,1,0:T(8,128)(2,1)S(1)} %multiply_convert_fusion) | copy-start | bytes 2752516
  193.1 3.4 %copy-start.15 = (f32[24]{0:T(128)S(1)}, f32[24]{0:T(128)}, u32[]{:S(2)}) copy-start(f32[24]{0:T(128)} %param.26) | copy-start | bytes 292
  193.1 4.2 %copy-start.17 = (f32[2,128]{1,0:T(2,128)S(1)}, f32[2,128]{1,0:T(2,128)}, u32[]{:S(2)}) copy-start(f32[2,128]{1,0:T(2,128)} %get-tuple-element.11) | copy-start | bytes 3076
  193.1 4.2 %copy-start.24 = (f32[24]{0:T(128)S(1)}, f32[24]{0:T(128)}, u32[]{:S(2)}) copy-start(f32[24]{0:T(128)} %exp.37) | copy-start | bytes 292
  193.1 5.4 %copy-start.16 = (pred[2,128]{1,0:T(4,128)(4,1)S(1)}, pred[2,128]{1,0:T(4,128)(4,1)}, u32[]{:S(2)}) copy-start(pred[2,128]{1,0:T(4,128)(4,1)} %get-tuple-element.10) | copy-start | bytes 772
  193.1 6.3 %copy-start = (f32[2,24,64,128]{3,2,1,0:T(8,128)S(1)}, f32[2,24,64,128]{3,2,1,0:T(8,128)}, u32[]{:S(2)}) copy-start(f32[2,24,64,128]{3,2,1,0:T(8,128)} %param.31) | copy-start | bytes 4718596
  197.3 3.0 %copy-start.2 = (bf16[2,128,1536]{1,2,0:T(8,128)(2,1)S(1)}, bf16[2,128,1536]{1,2,0:T(8,128)(2,1)}, u32[]{:S(2)}) copy-start(bf16[2,128,1536]{1,2,0:T(8,128)(2,1)} %copy.54) | copy-start | bytes 2359300
  197.4 3.0 %copy-start.23 = (f32[24]{0:T(128)S(1)}, f32[24]{0:T(128)}, u32[]{:S(2)}) copy-start(f32[24]{0:T(128)} %param.28) | copy-start | bytes 292
  203.9 1.3 copy-start.20
  205.2 5.3 %copy-start.19 = (pred[2,3]{1,0:T(4,128)(4,1)S(1)}, pred[2,3]{1,0:T(4,128)(4,1)}, u32[]{:S(2)}) copy-start(pred[2,3]{1,0:T(4,128)(4,1)} %compare_and_fusion) | copy-start | bytes 22
  211.5 13.4 %all-to-all-start.1 = ((bf16[2,24,192]{2,1,0:T(8,128)(2,1)}), bf16[2,24,192]{2,1,0:T(8,128)(2,1)S(1)}, u32[]{:S(2)}, u32[]{:S(2)}) async-start(bf16[2,24,192]{2,1,0:T(8,128)(2,1)} %convert_element_type.123), calls=%async_computation.2 | async-start | bytes 49152 | tf_op jit(solution)/shard_map/all_to_all | solution.py:151
  224.9 17.1 %copy-start.18 = (f32[128]{0:T(128)S(1)}, f32[128]{0:T(128)}, u32[]{:S(2)}) copy-start(f32[128]{0:T(128)} %compare_convert_fusion.1) | copy-start | bytes 1540
  224.9 15.8 %all-to-all-start = ((bf16[2,24,8192]{2,1,0:T(8,128)(2,1)}), bf16[2,24,8192]{2,1,0:T(8,128)(2,1)S(1)}, u32[]{:S(2)}, u32[]{:S(2)}) async-start(bf16[2,24,8192]{2,1,0:T(8,128)(2,1)} %convert_element_type.118), calls=%async_computation.1 | async-start | bytes 1572864 | tf_op jit(solution)/shard_map/all_to_all | solution.py:144
Sparse Core Ops, SparseCore 0:
  53.8 79.0 all-gather.1
  210.6 23.2 reduce-scatter.1
